TPU v7x, 256 devices: a whole 4x4x8 slice. The times are simulated.
256 devices in a mesh: chan: 16 (over x, z_lo), win: 16 (over z_hi, y, core).
Axes of the slice: x: 4, y: 4, z: 8 (z_hi: 2, z_lo: 4; z = z_hi * 4 + z_lo), core: 2. Of those that a mesh axis runs over, the one named last changes fastest.
Arguments:
- records: bfloat16 [64, 512, 1024], P('win', 'chan'), may hold values from -6 to 6
- live: int32 [512], P('chan'), may hold values 0 or 1
- band_limit: int32 [512], P('chan'), may hold values from 1 to 100
Outputs:
- correlations: float32 [512, 100, 257], P(('chan', 'win'))
Inputs may be any that keep to these rules, and one draw needn't show every extreme that they name: A pair of channel c with channel c + k is used for 1 <= k <= band_limit[c].
All inputs are finite; a program needn't handle non-finite values. No bound on the sum of `live` on one device may be relied on, other than what follows from the above.
Results may differ from a plain program's by a relative error of at most 0.0041.
Values may be sent and summed in bfloat16 or wider, within the bound.
A program may use at most 128 MiB of HBM per device.

v0:
```python
import math

import jax
import jax.numpy as jnp
import ml_dtypes
import numpy as np
from jax import lax
from jax.experimental import pallas as pl
from jax.experimental.pallas import tpu as pltpu
from jax.sharding import PartitionSpec as P

R = 100
LANES = 128
HALF_LAG = 128
HALF_WIN = 32
SAMPLES = 1024
BINS = SAMPLES // 2
LAGS = 2 * HALF_LAG + 1
WINS_ALL = 64
CHANNELS = 512

LAGS_PAD = 272
X, Z_LO, Z, YC = 4, 4, 8, 8
PLANE = Z * YC
SLICE = BINS // PLANE
EARLY = (LANES - R) // 4 * 4
BLOCKS = ((16, EARLY, 64), (64, 64, 96), (96, 96, 128))
ROWS = 2 * SLICE
REST = R - (Z_LO - 1) * 32

MESH = pl.DeviceIdType.MESH
F32, BF16 = jnp.float32, jnp.bfloat16


def split(table, terms):
    parts, rest = [], table.astype(np.float64)
    for _ in range(terms):
        part = rest.astype(np.float32).astype(ml_dtypes.bfloat16)
        parts.append(part)
        rest = rest - part.astype(np.float64)
    return parts


RESIDUES = (0, 4, 1, 7, 2, 6, 3, 5)
RUN = BINS // 8
ORDER = np.concatenate([np.arange(RUN) * 8 + (r or 8) for r in RESIDUES])


def forward_tables(terms):
    groups = []
    for g in range(4):
        halves = []
        for side in range(2):
            freqs = ORDER[(2 * g + side) * RUN:(2 * g + side + 1) * RUN, None]
            phase = np.mod(freqs * np.arange(LANES)[None, :], SAMPLES) * (2.0 * math.pi / SAMPLES)
            cos, sin = np.cos(phase), np.sin(phase)
            if g == 0:
                real, imag = [np.zeros_like(cos)] * 2, [np.zeros_like(cos)] * 2
                real[side], imag[side] = cos, -sin
            else:
                sign = 1 - 2 * side
                real, imag = [cos, sign * sin], [-sin, sign * cos]
            halves.append((np.concatenate(real, axis=1), np.concatenate(imag, axis=1)))
        (real_a, imag_a), (real_b, imag_b) = halves
        groups.append(np.concatenate([real_a, real_b, imag_a, imag_b], axis=0))
    return np.stack(split(np.stack(groups), terms))


def inverse_tables(terms):
    freqs = ORDER[:, None]
    shifts = np.arange(LAGS)[None, :] - HALF_LAG
    phase = np.mod(freqs * shifts, SAMPLES) * (2.0 * math.pi / SAMPLES)
    factor = 2.0 / math.sqrt(SAMPLES * WINS_ALL)
    real = (np.cos(phase) * factor).reshape(PLANE, SLICE, LAGS)
    imag = (-np.sin(phase) * factor).reshape(PLANE, SLICE, LAGS)
    table = np.concatenate([real, imag], axis=1).reshape(SAMPLES, LAGS).T
    table = np.pad(table, ((0, LAGS_PAD - LAGS), (0, 0)))
    return np.stack(split(table, terms))


def band_table():
    return (np.abs(ORDER[:, None] - ORDER[None, :]) <= HALF_WIN).astype(ml_dtypes.bfloat16)


def dot(a, b, dims):
    return lax.dot_general(a, b, (dims, ((), ())), preferred_element_type=F32)


def residue_sums(x):
    b = [x[:, LANES * i:LANES * (i + 1)].astype(F32) for i in range(8)]
    plus = [b[i] + b[i + 4] for i in range(4)]
    minus = [b[i] - b[i + 4] for i in range(4)]
    even, odd = plus[0] + plus[2], plus[1] + plus[3]
    root = math.sqrt(0.5)
    across, along = (minus[1] - minus[3]) * root, (minus[1] + minus[3]) * root
    return (
        (even + odd, even - odd),
        (minus[0] + across, -minus[2] - along),
        (plus[0] - plus[2], plus[3] - plus[1]),
        (minus[0] - across, minus[2] - along),
    )


def whiten(x, live, tab_ref, band):
    real, imag = [], []
    for g, sums in enumerate(residue_sums(x)):
        sums = jnp.concatenate(sums, axis=1)
        high = sums.astype(BF16)
        low = (sums - high.astype(F32)).astype(BF16)
        spec = dot(tab_ref[0, g], high, ((1,), (1,)))
        spec = spec + dot(tab_ref[0, g], low, ((1,), (1,)))
        spec = spec + dot(tab_ref[1, g], high, ((1,), (1,)))
        real.append(spec[:2 * RUN])
        imag.append(spec[2 * RUN:])
    real, imag = jnp.concatenate(real, axis=0), jnp.concatenate(imag, axis=0)
    amplitude = jnp.sqrt(real * real + imag * imag)
    high = amplitude.astype(BF16)
    low = (amplitude - high.astype(F32)).astype(BF16)
    near = dot(band, high, ((1,), (0,))) + dot(band, low, ((1,), (0,)))
    factor = live / (near * (1.0 / (2 * HALF_WIN + 1)) + 1e-06)
    real = (real * factor).reshape(PLANE, SLICE, LANES)
    imag = (imag * factor).reshape(PLANE, SLICE, LANES)
    return jnp.concatenate([real, imag], axis=1).astype(BF16)


def regroup(parts):
    group = lax.broadcasted_iota(jnp.int32, parts[0].shape, 1) // 32
    for bit in range(2):
        step = 32 << bit
        upper = (group // (1 << bit)) % 2 == 1
        new = list(parts)
        for i in range(4):
            if i & (1 << bit):
                continue
            a, b = parts[i], parts[i | (1 << bit)]
            new[i] = jnp.where(upper, pltpu.roll(b, step, 1), a)
            new[i | (1 << bit)] = jnp.where(upper, b, pltpu.roll(a, LANES - step, 1))
        parts = new
    return parts


def regroup_plane(ref, t_ref, plane, rest_ref=None):
    def take(s, _):
        from_z = lax.div(s, YC) * (Z_LO * YC) + lax.rem(s, YC)
        if rest_ref is None:
            parts = [ref[from_z + z * YC] for z in range(Z_LO)]
        else:
            parts = [ref[from_z + z * YC] for z in range(Z_LO - 1)]
            shift = lax.rem(LANES - REST * lax.rem(s, YC), LANES)
            parts.append(pltpu.roll(rest_ref[lax.div(s, YC)], shift, 1))
        parts = [part.astype(F32) for part in regroup(parts)]
        for w in range(4):
            at = pl.ds(pl.multiple_of((s * 4 + w) * SLICE, SLICE), SLICE)
            t_ref[plane, 0, at] = parts[w][:SLICE]
            t_ref[plane, 1, at] = parts[w][SLICE:]
        return 0

    lax.fori_loop(0, 2 * YC, take, 0, unroll=16)


def columns(t_ref, plane, f):
    every = pl.ds(f, WINS_ALL, stride=SLICE)
    re, im = t_ref[plane, 0, every], t_ref[plane, 1, every]
    own = jnp.concatenate([re, im], axis=0)
    turned = jnp.concatenate([-im, re], axis=0)
    return own, jnp.concatenate([own, turned], axis=1).astype(BF16)


def gather_rest(near_ref, rest_ref):
    place = lax.broadcasted_iota(jnp.int32, (ROWS, LANES), 1) % 32 // REST
    for high in range(2):
        first = (high * Z_LO + Z_LO - 1) * YC
        rest = near_ref[first]
        for from_yc in range(1, YC):
            rest = jnp.where(place == from_yc, pltpu.roll(near_ref[first + from_yc], REST * from_yc, 1), rest)
        rest_ref[high] = rest


def near_pairs(t_ref, u_ref, left_ref):
    for f in range(SLICE):
        own, both = columns(t_ref, 0, f)
        left = own.T.astype(BF16)
        left_ref[f] = left
        pairs = dot(left, both, ((1,), (0,)))
        for part in range(2):
            u_ref[pl.ds(part * SLICE + f, LANES, stride=ROWS)] = pairs[:, part * LANES:(part + 1) * LANES]


def far_pairs(t_ref, u_ref, left_ref, both_ref, start, end, first):
    rows = lax.broadcasted_iota(jnp.int32, (end - start, LANES), 0) + start
    near = lax.broadcasted_iota(jnp.int32, (end - start, LANES), 1) > rows
    for f in range(SLICE):
        if first:
            both_ref[f] = columns(t_ref, 1, f)[1]
        pairs = dot(left_ref[f, start:end], both_ref[f], ((1,), (0,)))
        for part in range(2):
            at = pl.ds(start * ROWS + part * SLICE + f, end - start, stride=ROWS)
            u_ref[at] = jnp.where(near, u_ref[at], pairs[:, part * LANES:(part + 1) * LANES])


def round_rows(u_ref, s_ref, start, end):
    done = u_ref[start * ROWS:end * ROWS]
    s_ref[start // 2:end // 2] = done.astype(BF16).reshape((end - start) // 2, 2, ROWS, LANES)


def kernel(limit_hbm, live_hbm, x_hbm, tab_hbm, band_hbm, itab_hbm, out_ref,
           limit_ref, live_ref, x_ref, tab_ref, band_ref, itab_ref, w_ref, near_ref, far_ref, near_rest_ref, far_rest_ref, t_ref, u_ref, left_ref, both_ref, s_ref, got_ref,
           local_sem, send_sem, near_sem, far_sem, got_sem, rest_sem, ready_sem):
    chan, win = lax.axis_index("chan"), lax.axis_index("win")
    x = lax.div(chan, Z_LO)
    z, yc = lax.div(win, YC) * Z_LO + lax.rem(chan, Z_LO), lax.rem(win, YC)
    me = z * YC + yc
    has_left, has_right = x > 0, x < X - 1

    def device(to_x, to_z, to_yc):
        return {"chan": to_x * Z_LO + lax.rem(to_z, Z_LO), "win": lax.div(to_z, Z_LO) * YC + to_yc}

    loads = [
        pltpu.make_async_copy(src, dst, local_sem.at[i])
        for i, (src, dst) in enumerate(
            ((live_hbm, live_ref), (x_hbm, x_ref), (tab_hbm, tab_ref), (band_hbm, band_ref),
             (itab_hbm, itab_ref), (limit_hbm, limit_ref)))
    ]
    for load in loads[:4]:
        load.start()

    barrier = pltpu.get_barrier_semaphore()

    def signal(semaphore, to):
        pl.semaphore_signal(semaphore, inc=1, device_id=to, device_id_type=MESH)

    for step in range(1, Z):
        signal(barrier, device(x, lax.rem(z + step, Z), yc))
    for step in range(1, YC):
        signal(barrier, device(x, z, lax.rem(yc + step, YC)))

    @pl.when(has_right)
    def _():
        signal(barrier, device(x + 1, z, yc))

    for load in loads[4:]:
        load.start()
    lane = lax.rem(lax.broadcasted_iota(jnp.int32, (1, LANES), 1), 32)
    live = jnp.zeros((1, LANES), F32)
    loads[0].wait()
    for c in range(32):
        live = jnp.where(lane == c, live_ref[c].astype(F32), live)
    for load in loads[1:4]:
        load.wait()
    w_ref[...] = whiten(x_ref[...], live, tab_ref, band_ref[...])

    pl.semaphore_wait(barrier, Z - 1 + YC - 1 + has_left.astype(jnp.int32))
    for step in range(1, YC):
        signal(ready_sem, device(x, z, lax.rem(yc + step, YC)))

    own = pltpu.make_async_copy(w_ref.at[me], near_ref.at[me], local_sem.at[6])
    own.start()
    order = (0, 1, 7, 2, 6, 3, 5, 4)

    def send(to_z, to_yc):
        pltpu.make_async_remote_copy(
            src_ref=w_ref.at[to_z * YC + to_yc], dst_ref=near_ref.at[me], send_sem=send_sem,
            recv_sem=near_sem.at[z], device_id=device(x, to_z, to_yc), device_id_type=MESH,
        ).start()

    for step in order[1:]:
        send(lax.rem(z + step, Z), yc)
    for step in range(1, YC):
        send(z, lax.rem(yc + step, YC))
    pl.semaphore_wait(ready_sem, YC - 1)
    for step in order[1:]:
        to_z = lax.rem(z + step, Z)

        def send_on(i, _, to_z=to_z):
            send(to_z, lax.rem(yc + i, YC))
            return 0

        lax.fori_loop(1, YC, send_on, 0)

    @pl.when(jnp.logical_not(has_right))
    def _():
        far_ref[...] = jnp.zeros_like(far_ref)
        far_rest_ref[...] = jnp.zeros_like(far_rest_ref)

    own.wait()
    for step in order:
        from_z = lax.rem(z + Z - step, Z)
        chunk = pl.ds(from_z * YC, YC)
        some = near_ref.at[pl.ds(0, YC if step else YC - 1)]
        pltpu.make_async_copy(some, some, near_sem.at[from_z]).wait()

        @pl.when(jnp.logical_and(has_left, lax.rem(from_z, Z_LO) != Z_LO - 1))
        def _(chunk=chunk):
            pltpu.make_async_remote_copy(
                src_ref=near_ref.at[chunk], dst_ref=far_ref.at[chunk], send_sem=send_sem,
                recv_sem=far_sem, device_id=device(x - 1, z, yc), device_id_type=MESH,
            ).start()

    @pl.when(has_left)
    def _():
        gather_rest(near_ref, near_rest_ref)
        pltpu.make_async_remote_copy(
            src_ref=near_rest_ref, dst_ref=far_rest_ref, send_sem=send_sem,
            recv_sem=rest_sem, device_id=device(x - 1, z, yc), device_id_type=MESH,
        ).start()

    def give(start, end):
        round_rows(u_ref, s_ref, start, end)
        first, count = start // 2, (end - start) // 2

        def go(i, _):
            pair = first + lax.rem(i + z * 2 + yc, count)
            to_z = lax.div(lax.rem(pair, 2 * YC), YC) * Z_LO + lax.div(pair, 2 * YC)
            to_yc = lax.rem(pair, YC)

            @pl.when(to_z * YC + to_yc != me)
            def _():
                pltpu.make_async_remote_copy(
                    src_ref=s_ref.at[pair], dst_ref=got_ref.at[me], send_sem=send_sem,
                    recv_sem=got_sem, device_id=device(x, to_z, to_yc), device_id_type=MESH,
                ).start()
            return 0

        lax.fori_loop(0, count, go, 0)

    regroup_plane(near_ref, t_ref, 0)
    near_pairs(t_ref, u_ref, left_ref)
    give(0, EARLY)

    @pl.when(has_right)
    def _():
        whole = far_ref.at[pl.ds(0, 2 * (Z_LO - 1) * YC)]
        pltpu.make_async_copy(whole, whole, far_sem).wait()
        pltpu.make_async_copy(far_rest_ref, far_rest_ref, rest_sem).wait()

    regroup_plane(far_ref, t_ref, 1, far_rest_ref)
    for start, send_start, end in BLOCKS:
        far_pairs(t_ref, u_ref, left_ref, both_ref, start, end, start == BLOCKS[0][0])
        give(send_start, end)

    owned = lax.rem(z, Z_LO) * (2 * YC) + lax.div(z, Z_LO) * YC + yc
    own = pltpu.make_async_copy(s_ref.at[owned], got_ref.at[me], local_sem.at[7])
    own.start()
    own.wait()
    loads[4].wait()
    loads[5].wait()
    rest = got_ref.at[pl.ds(0, PLANE - 1)]
    pltpu.make_async_copy(rest, rest, got_sem).wait()

    right = jnp.concatenate([got_ref[:, c].reshape(SAMPLES, LANES) for c in range(2)], axis=1)
    pairs = dot(itab_ref[0], right, ((1,), (0,)))
    for term in range(1, itab_ref.shape[0]):
        pairs = pairs + dot(itab_ref[term], right, ((1,), (0,)))
    offsets = lax.broadcasted_iota(jnp.int32, (LAGS_PAD, LANES), 1) + 1
    first = lax.rem(chan, Z_LO) * 32 + win * 2
    for c in range(2):
        reach = jnp.minimum(limit_ref[win * 2 + c], CHANNELS - 1 - (chan * 32 + win * 2 + c))
        kept = pltpu.roll(pairs[:, c * LANES:(c + 1) * LANES], LANES - 1 - c - first, 1)
        out_ref[pl.ds(c, LAGS_PAD, stride=2)] = jnp.where(offsets <= reach, kept, 0.0)

    sent = w_ref.at[pl.ds(0, PLANE - 1)]
    pltpu.make_async_copy(sent, sent, send_sem).wait()
    pltpu.make_async_copy(rest, rest, send_sem).wait()

    @pl.when(has_left)
    def _():
        whole = far_ref.at[pl.ds(0, 2 * (Z_LO - 1) * YC)]
        pltpu.make_async_copy(whole, whole, send_sem).wait()
        pltpu.make_async_copy(near_rest_ref, near_rest_ref, send_sem).wait()


def shards(records, live, band_limit):
    tab = jnp.asarray(forward_tables(2))
    band = jnp.asarray(band_table())
    itab = jnp.asarray(inverse_tables(2))
    rows = records.reshape(LANES, SAMPLES)
    vmem, hbm = pl.BlockSpec(memory_space=pltpu.VMEM), pl.BlockSpec(memory_space=pltpu.HBM)
    out = pl.pallas_call(
        kernel,
        out_shape=jax.ShapeDtypeStruct((2 * LAGS_PAD, LANES), F32),
        in_specs=[hbm] * 6,
        out_specs=vmem,
        scratch_shapes=[
            pltpu.SMEM(band_limit.shape, jnp.int32),
            pltpu.SMEM(live.shape, jnp.int32),
            pltpu.VMEM(rows.shape, BF16),
            pltpu.VMEM(tab.shape, BF16),
            pltpu.VMEM(band.shape, BF16),
            pltpu.VMEM(itab.shape, BF16),
            pltpu.VMEM((PLANE, ROWS, LANES), BF16),
            pltpu.VMEM((PLANE, ROWS, LANES), BF16),
            pltpu.VMEM((PLANE, ROWS, LANES), BF16),
            pltpu.VMEM((2, ROWS, LANES), BF16),
            pltpu.VMEM((2, ROWS, LANES), BF16),
            pltpu.VMEM((2, 2, WINS_ALL * SLICE, LANES), F32),
            pltpu.VMEM((LANES * ROWS, LANES), F32),
            pltpu.VMEM((SLICE, LANES, LANES), BF16),
            pltpu.VMEM((SLICE, LANES, 2 * LANES), BF16),
            pltpu.VMEM((PLANE, 2, ROWS, LANES), BF16),
            pltpu.VMEM((PLANE, 2, ROWS, LANES), BF16),
            pltpu.SemaphoreType.DMA((8,)),
            pltpu.SemaphoreType.DMA,
            pltpu.SemaphoreType.DMA((Z,)),
            pltpu.SemaphoreType.DMA,
            pltpu.SemaphoreType.DMA,
            pltpu.SemaphoreType.DMA,
            pltpu.SemaphoreType.REGULAR,
        ],
        compiler_params=pltpu.CompilerParams(
            collective_id=0, has_side_effects=True, vmem_limit_bytes=40 << 20
        ),
        cost_estimate=pl.CostEstimate(flops=1_500_000_000, bytes_accessed=8_000_000, transcendentals=65536),
        name="correlate",
    )(*[pltpu.with_memory_space_constraint(a, pltpu.HBM) for a in (band_limit, live, rows, tab, band, itab)])
    out = out.reshape(LAGS_PAD, 2, LANES)[:LAGS, :, :R]
    return jnp.transpose(out, (1, 2, 0))


def solution(mesh):
    placed = (P("win", "chan", None), P("chan"), P("chan"))
    return jax.shard_map(
        shards,
        mesh=mesh,
        in_specs=placed,
        out_specs=P(("chan", "win"), None, None),
        check_vma=False,
    )
```

profile of v0, /device:TPU:97, one launch (start us, length us, event | category | flops | bytes accessed | tf_op | source)
XLA Modules:
  0.0 37.0 jit_solution(3779060547905648069)
XLA Ops:
  0.0 36.3 %correlate.1 = f32[544,128]{1,0:T(8,128)S(1)} custom-call(s32[32]{0:T(128)} %limit_hbm.1, s32[32]{0:T(128)} %live_hbm.1, bf16[128,1024]{1,0:T(8,128)(2,1)} %bitcast.5, bf16[2,4,256,256]{3,2,1,0:T(8,128)(2,1)} %constant.6.clone.tab_hbm, bf16[512,512]{1,0:T(8,128)(2,1)} %constant.7.clone.band_hbm, bf16[2,272,1024]{2,1,0:T(8,128)(2,1)} %constant.8.clone.itab_hbm), custom_call_target="tpu_custom_call" | custom-call | flops 1500000000 | bytes 8000000 | tf_op jit(solution)/shard_map/correlate/pallas_call | solution.py:378
  36.3 0.7 %slice_bitcast_fusion = f32[2,100,257]{1,0,2:T(2,128)} fusion(f32[272,2,128]{2,1,0:T(2,128)S(1)} %bitcast.4), kind=kLoop, calls=%fused_computation | loop fusion | bytes 411200 | tf_op jit(solution)/shard_map/transpose | solution.py:416
where the time goes:
time: 37.1 us; the launch traced here: 37 us
  Pallas kernels  36.3 us (98%)
  local copies, waits for them, and re-layouts  0.72 us (2%)
    pallas_call x1, Pallas kernels, shards(): pl.pallas_call(kernel, out_shape=jax.ShapeDtypeStruct((2 * LAGS_PAD, LANE...  36.3 us

commit v1 on v0

--- a/solution.py
+++ b/solution.py
@@ -356,7 +356,7 @@
     for c in range(2):
         reach = jnp.minimum(limit_ref[win * 2 + c], CHANNELS - 1 - (chan * 32 + win * 2 + c))
         kept = pltpu.roll(pairs[:, c * LANES:(c + 1) * LANES], LANES - 1 - c - first, 1)
-        out_ref[pl.ds(c, LAGS_PAD, stride=2)] = jnp.where(offsets <= reach, kept, 0.0)
+        out_ref[pl.ds(c, LAGS_PAD - 8, stride=2)] = jnp.where(offsets <= reach, kept, 0.0)[:LAGS_PAD - 8]
 
     sent = w_ref.at[pl.ds(0, PLANE - 1)]
     pltpu.make_async_copy(sent, sent, send_sem).wait()
@@ -392,8 +392,8 @@
             pltpu.VMEM((PLANE, ROWS, LANES), BF16),
             pltpu.VMEM((2, ROWS, LANES), BF16),
             pltpu.VMEM((2, ROWS, LANES), BF16),
-            pltpu.VMEM((2, 2, WINS_ALL * SLICE, LANES), F32),
-            pltpu.VMEM((LANES * ROWS, LANES), F32),
+            pltpu.VMEM((2, 2, (WINS_ALL + 1) * SLICE, LANES), F32),
+            pltpu.VMEM(((LANES + 1) * ROWS, LANES), F32),
             pltpu.VMEM((SLICE, LANES, LANES), BF16),
             pltpu.VMEM((SLICE, LANES, 2 * LANES), BF16),
             pltpu.VMEM((PLANE, 2, ROWS, LANES), BF16),

time: 37.1 us -> 37.1 us (level)
  no operation moved by 1% of the time
where the time goes in v1:
time: 37.1 us; the launch traced here: 37 us
  Pallas kernels  36.3 us (98%)
  local copies, waits for them, and re-layouts  0.72 us (2%)
    pallas_call x1, Pallas kernels, shards(): pl.pallas_call(kernel, out_shape=jax.ShapeDtypeStruct((2 * LAGS_PAD, LANE...  36.3 us

profile of v1, /device:TPU:97, one launch (start us, length us, event | category | flops | bytes accessed | tf_op | source)
XLA Modules:
  0.0 37.0 jit_solution(10862615711321508300)
XLA Ops:
  0.0 36.3 %correlate.1 = f32[544,128]{1,0:T(8,128)S(1)} custom-call(s32[32]{0:T(128)} %limit_hbm.1, s32[32]{0:T(128)} %live_hbm.1, bf16[128,1024]{1,0:T(8,128)(2,1)} %bitcast.5, bf16[2,4,256,256]{3,2,1,0:T(8,128)(2,1)} %constant.6.clone.tab_hbm, bf16[512,512]{1,0:T(8,128)(2,1)} %constant.7.clone.band_hbm, bf16[2,272,1024]{2,1,0:T(8,128)(2,1)} %constant.8.clone.itab_hbm), custom_call_target="tpu_custom_call" | custom-call | flops 1500000000 | bytes 8000000 | tf_op jit(solution)/shard_map/correlate/pallas_call | solution.py:378
  36.3 0.7 %slice_bitcast_fusion = f32[2,100,257]{1,0,2:T(2,128)} fusion(f32[272,2,128]{2,1,0:T(2,128)S(1)} %bitcast.4), kind=kLoop, calls=%fused_computation | loop fusion | bytes 411200 | tf_op jit(solution)/shard_map/transpose | solution.py:416

commit v2 on v1

--- a/solution.py
+++ b/solution.py
@@ -321,7 +321,7 @@
                 ).start()
             return 0
 
-        lax.fori_loop(0, count, go, 0)
+        lax.fori_loop(0, count, go, 0, unroll=2)
 
     regroup_plane(near_ref, t_ref, 0)
     near_pairs(t_ref, u_ref, left_ref)

time: 37.1 us -> 37.1 us (level)
  no operation moved by 1% of the time
where the time goes in v2:
time: 37.1 us; the launch traced here: 37 us
  Pallas kernels  36.3 us (98%)
  local copies, waits for them, and re-layouts  0.72 us (2%)
    pallas_call x1, Pallas kernels, shards(): pl.pallas_call(kernel, out_shape=jax.ShapeDtypeStruct((2 * LAGS_PAD, LANE...  36.3 us

profile of v2, /device:TPU:97, one launch (start us, length us, event | category | flops | bytes accessed | tf_op | source)
XLA Modules:
  0.0 37.0 jit_solution(13958574924087688622)
XLA Ops:
  0.0 36.3 %correlate.1 = f32[544,128]{1,0:T(8,128)S(1)} custom-call(s32[32]{0:T(128)} %limit_hbm.1, s32[32]{0:T(128)} %live_hbm.1, bf16[128,1024]{1,0:T(8,128)(2,1)} %bitcast.5, bf16[2,4,256,256]{3,2,1,0:T(8,128)(2,1)} %constant.6.clone.tab_hbm, bf16[512,512]{1,0:T(8,128)(2,1)} %constant.7.clone.band_hbm, bf16[2,272,1024]{2,1,0:T(8,128)(2,1)} %constant.8.clone.itab_hbm), custom_call_target="tpu_custom_call" | custom-call | flops 1500000000 | bytes 8000000 | tf_op jit(solution)/shard_map/correlate/pallas_call | solution.py:378
  36.3 0.7 %slice_bitcast_fusion = f32[2,100,257]{1,0,2:T(2,128)} fusion(f32[272,2,128]{2,1,0:T(2,128)S(1)} %bitcast.4), kind=kLoop, calls=%fused_computation | loop fusion | bytes 411200 | tf_op jit(solution)/shard_map/transpose | solution.py:416
